TPU v7x, 128 devices: a whole 4x4x4 slice. The times are simulated.
128 devices in a mesh: dp: 32 (over y, z, x_hi), mp: 4 (over x_lo, core).
Axes of the slice: x: 4 (x_hi: 2, x_lo: 2; x = x_hi * 2 + x_lo), y: 4, z: 4, core: 2. Of those that a mesh axis runs over, the one named last changes fastest.
Arguments:
- student: bfloat16 [2048, 16, 1280], P('dp'), may hold values from -6 to 6
- dino_target: bfloat16 [1024, 16, 1536], P('dp', None, 'mp'), may hold values from -6 to 6
- siglip_target: bfloat16 [1024, 16, 1152], P('dp', None, 'mp'), may hold values from -6 to 6
- clip_target: bfloat16 [1024, 16, 1024], P('dp', None, 'mp'), may hold values from -6 to 6
- image_owner: int32 [1024, 1], replicated, may hold values from 0 to 31; in each aligned block of 32 rows (0 to 31, 32 to 63, ...) at most 2 rows name the same one
- patch_count: int32 [1024], replicated, may hold values from 1 to 16
- dino_expand: bfloat16 [1280, 1536], P(None, 'mp'), may hold values from -0.15625 to 0.15625
- dino_project: bfloat16 [1536, 1536], P('mp'), may hold values from -0.15625 to 0.15625
- siglip_expand: bfloat16 [1280, 1536], P(None, 'mp'), may hold values from -0.15625 to 0.15625
- siglip_project: bfloat16 [1536, 1152], P('mp'), may hold values from -0.15625 to 0.15625
- clip_expand: bfloat16 [1280, 1536], P(None, 'mp'), may hold values from -0.15625 to 0.15625
- clip_project: bfloat16 [1536, 1024], P('mp'), may hold values from -0.15625 to 0.15625
Outputs:
- student_grad: bfloat16 [2048, 16, 1280], P('dp', None, 'mp')
- dino_expand_grad: float32 [1280, 1536], P('dp', 'mp')
- dino_project_grad: float32 [1536, 1536], P('mp', 'dp')
- siglip_expand_grad: float32 [1280, 1536], P('dp', 'mp')
- siglip_project_grad: float32 [1536, 1152], P('mp', 'dp')
- clip_expand_grad: float32 [1280, 1536], P('dp', 'mp')
- clip_project_grad: float32 [1536, 1024], P('mp', 'dp')
Inputs may be any that keep to these rules, and one draw needn't show every extreme that they name: `image_owner`: within each aligned block of 32 images (one store shard) no owner is named more than 2 times; every owner is named by some image.
All inputs are finite; a program needn't handle non-finite values.
Results may differ from a plain program's by a relative error of at most 0.028.
Values may be sent and summed in bfloat16 or wider, within the bound.
No kernel may reach another device: no remote copies, remote signals or barrier semaphores. Data moves between devices by JAX's collectives and lax.ppermute only.
A program may use at most 128 MiB of HBM per device.

v0:
```python
import jax
import jax.numpy as jnp
from jax import lax
from jax.sharding import PartitionSpec as P


def for_sending(value):

    def short(part):
        return part.astype(jnp.bfloat16) if part.dtype == jnp.float32 else part

    return jax.tree.map(short, value)


def gelu_parts(hidden):
    normal_cdf = 0.5 * (1.0 + jax.scipy.special.erf(hidden * 0.7071067811865476))
    density = jnp.exp(-0.5 * hidden * hidden) * 0.3989422804014327
    return (hidden * normal_cdf, normal_cdf + hidden * density)


def selection(store_block, owner_ids, capacity):
    belongs = (owner_ids[:, None] == store_block[None, :]).astype(jnp.int32)
    position = jnp.cumsum(belongs, axis=1) - 1
    ranks = jnp.arange(capacity, dtype=jnp.int32)
    return belongs[:, None, :] * (position[:, None, :] == ranks[None, :, None]).astype(jnp.int32)


def fold_step(activated, project, segment):
    back_sum = lax.dot_general(
        segment, project, (((1,), (1,)), ((), ())), preferred_element_type=jnp.float32
    )
    update = lax.dot_general(
        activated, segment, (((0,), (0,)), ((), ())), preferred_element_type=jnp.float32
    )
    return (back_sum, update)


def first_term(inputs, hidden_grad, loss_scale):
    return (
        lax.dot_general(
            inputs, hidden_grad, (((0,), (0,)), ((), ())), preferred_element_type=jnp.float32
        )
        * loss_scale
    )


def adapt(inputs, targets, slot_counts, weights, loss_scale):
    positions = jnp.arange(targets[0].shape[2], dtype=jnp.int32)
    valid_mask = (
        (positions[None, None, :] < slot_counts[:, :, None]).astype(jnp.float32).reshape(-1)
    )
    student_part = jnp.zeros(inputs.shape, jnp.float32)
    results = []
    for target, weight_pair in zip(targets, weights):
        expand, project = weight_pair
        hidden = jnp.dot(inputs, expand, preferred_element_type=jnp.float32)
        activated, gelu_slope = gelu_parts(hidden)
        activated = activated.astype(jnp.bfloat16)
        adapted = lax.psum_scatter(
            jnp.dot(activated, project, preferred_element_type=jnp.float32).astype(jnp.bfloat16),
            "mp",
            scatter_dimension=1,
            tiled=True,
        ).astype(jnp.float32)
        target_flat = target.reshape(-1, target.shape[3]).astype(jnp.float32)
        residual = ((adapted - target_flat) * valid_mask[:, None]).astype(jnp.bfloat16)
        back_sum, project_grad = fold_step(
            activated, project, lax.all_gather(residual, "mp", axis=1, tiled=True)
        )
        hidden_grad = (back_sum * gelu_slope).astype(jnp.bfloat16)
        expand_grad = lax.psum_scatter(
            first_term(inputs, hidden_grad, loss_scale).astype(jnp.bfloat16),
            "dp",
            scatter_dimension=0,
            tiled=True,
        ).astype(jnp.float32)
        project_grad = lax.psum_scatter(
            (project_grad * loss_scale).astype(jnp.bfloat16), "dp", scatter_dimension=1, tiled=True
        ).astype(jnp.float32)
        student_part = student_part + lax.dot_general(
            hidden_grad, expand, (((1,), (1,)), ((), ())), preferred_element_type=jnp.float32
        )
        results.append(expand_grad)
        results.append(project_grad)
    return (student_part, results)


def shards(
    student,
    dino_target,
    siglip_target,
    clip_target,
    image_owner,
    patch_count,
    dino_expand,
    dino_project,
    siglip_expand,
    siglip_project,
    clip_expand,
    clip_project,
):
    stores = lax.axis_size("dp")
    store_index = lax.axis_index("dp")
    per_store = dino_target.shape[0]
    patches = dino_target.shape[1]
    slot_total = student.shape[0]
    capacity = slot_total // stores
    owners = image_owner[:, 0]
    store_owner = owners.reshape(stores, per_store)
    counts_store = patch_count.reshape(stores, per_store)
    loss_scale = 1.0 / jnp.sqrt(jnp.sum(patch_count).astype(jnp.float32))
    own_block = lax.dynamic_slice_in_dim(owners, store_index * per_store, per_store)
    sel_store = selection(own_block, jnp.arange(stores, dtype=jnp.int32), capacity)
    picker = sel_store.astype(jnp.bfloat16)
    teachers = (dino_target, siglip_target, clip_target)
    weights = (
        (dino_expand, dino_project),
        (siglip_expand, siglip_project),
        (clip_expand, clip_project),
    )
    outgoing = tuple(
        (
            jnp.einsum("oki,ipf->okpf", picker, teacher, preferred_element_type=jnp.float32).astype(
                jnp.bfloat16
            )
            for teacher in teachers
        )
    )
    targets = jax.tree.map(
        lambda part, own: part.astype(own.dtype),
        lax.all_to_all(for_sending(outgoing), "dp", split_axis=0, concat_axis=0, tiled=True),
        outgoing,
    )
    owner_key = jnp.reshape(store_index, (1,))
    sel_owner = jax.vmap(lambda store_block: selection(store_block, owner_key, capacity)[0])(
        store_owner
    )
    slot_counts = jnp.sum(sel_owner * counts_store[:, None, :], axis=2)
    inputs = student.reshape(-1, student.shape[2])
    student_part, results = adapt(inputs, targets, slot_counts, weights, loss_scale)
    student_grad = lax.psum_scatter(
        student_part.reshape(slot_total, patches, -1).astype(jnp.bfloat16),
        "mp",
        scatter_dimension=2,
        tiled=True,
    )
    return (student_grad, results[0], results[1], results[2], results[3], results[4], results[5])


def solution(mesh):
    return jax.shard_map(
        shards,
        mesh=mesh,
        in_specs=(
            P("dp", None, None),
            P("dp", None, "mp"),
            P("dp", None, "mp"),
            P("dp", None, "mp"),
            P(),
            P(),
            P(None, "mp"),
            P("mp", None),
            P(None, "mp"),
            P("mp", None),
            P(None, "mp"),
            P("mp", None),
        ),
        out_specs=(
            P("dp", None, "mp"),
            P("dp", "mp"),
            P("mp", "dp"),
            P("dp", "mp"),
            P("mp", "dp"),
            P("dp", "mp"),
            P("mp", "dp"),
        ),
        check_vma=False,
    )
```

profile of v0, /device:TPU:1, one launch (start us, length us, event | category | flops | bytes accessed | tf_op | source)
XLA Modules:
  0.0 1115.3 jit_solution(8419298661973129397)
XLA Ops:
  7.2 1.7 copy-done
  8.9 3.9 multiply_convert_fusion.1
  13.7 2.6 convolution_convert_fusion.2
  16.5 2.8 fusion.56
  19.3 1.2 copy-done.23
  20.4 3.5 convolution_convert_fusion.1
  24.0 4.7 copy.50
  28.7 4.0 multiply_convert_fusion.2
  32.7 0.9 copy-done.21
  33.6 2.9 convolution_convert_fusion
  37.8 1.1 copy.45
  38.9 11.4 %all-to-all-start.2 = ((bf16[32,2,16,256]{3,2,1,0:T(8,128)(2,1)}), bf16[32,2,16,256]{3,2,1,0:T(8,128)(2,1)S(1)}, u32[]{:S(2)}, u32[]{:S(2)}) async-start(bf16[32,2,16,256]{3,2,1,0:T(8,128)(2,1)} %copy.45), calls=%async_computation.4 | async-start | bytes 1048576 | tf_op jit(solution)/shard_map/all_to_all | solution.py:131
  51.1 11.7 %all-to-all-done.2 = bf16[32,2,16,256]{3,2,1,0:T(8,128)(2,1)S(1)} async-done(((bf16[32,2,16,256]{3,2,1,0:T(8,128)(2,1)}), bf16[32,2,16,256]{3,2,1,0:T(8,128)(2,1)S(1)}, u32[]{:S(2)}, u32[]{:S(2)}) %all-to-all-start.2) | async-done | bytes 524320 | tf_op jit(solution)/shard_map/all_to_all | solution.py:131
  62.9 2.0 fusion.30
  64.9 1.4 convolution_convert_fusion.4
  66.3 1.2 copy.39
  67.5 3.9 all-to-all-start
  71.5 25.6 %reduce-scatter.24.cloned.1.call-done = bf16[384,1024]{1,0:T(8,128)(2,1)} async-done(((bf16[1536,1024]{1,0:T(8,128)(2,1)}), bf16[384,1024]{1,0:T(8,128)(2,1)}) %reduce-scatter.24.cloned.1.call-update) | async-done | bytes 786448
  97.1 2.3 copy.51
  99.4 2.3 fusion.28
  101.7 1.3 convolution_convert_fusion.3
  103.3 33.6 %all_to_all.15 = bf16[32,2,16,288]{3,2,1,0:T(8,128)(2,1)S(1)} all-to-all(bf16[32,2,16,288]{3,2,1,0:T(8,128)(2,1)S(1)} %copy.42), channel_id=1, replica_groups=mesh['dp'=32,'mp'=4] {'dp'}, dimensions={0} | all-to-all | bytes 1179648 | tf_op jit(solution)/shard_map/all_to_all | solution.py:131
  136.9 1.3 bitcast_convert_fusion
  138.3 2.9 copy.43
  141.2 2.5 multiply_convert_fusion.4
  145.3 25.7 %all-gather.8.cloned.1.call-done = bf16[1024,1024]{1,0:T(8,128)(2,1)} async-done(((bf16[1024,256]{1,0:T(8,128)(2,1)}), bf16[1024,1024]{1,0:T(8,128)(2,1)}) %all-gather.8.cloned.1.call-update) | async-done | bytes 2097168 | tf_op jit(solution)/shard_map/all_gather | solution.py:68
  171.1 3.8 multiply_convert_fusion
  174.9 37.0 %all-gather.4.cloned.1.call-done = bf16[1024,1536]{1,0:T(8,128)(2,1)} async-done(((bf16[1024,384]{1,0:T(8,128)(2,1)}), bf16[1024,1536]{1,0:T(8,128)(2,1)}) %all-gather.4.cloned.1.call-update) | async-done | bytes 3145744 | tf_op jit(solution)/shard_map/all_gather | solution.py:68
  212.0 5.3 fusion.1
  217.3 3.6 fusion.26
  221.8 2.2 fusion.6
  224.0 21.8 %all-gather.6.cloned.1.call-done = bf16[1024,1152]{0,1:T(8,128)(2,1)} async-done(((bf16[1024,288]{0,1:T(8,128)(2,1)}), bf16[1024,1152]{0,1:T(8,128)(2,1)}) %all-gather.6.cloned.1.call-update) | async-done | bytes 2359312 | tf_op jit(solution)/shard_map/all_gather | solution.py:68
  245.8 4.3 fusion.20
  250.1 2.2 fusion.7
  252.4 2.1 fusion.14
  255.4 2.2 fusion.8
  257.9 0.9 copy-done.7
  258.8 1.5 fusion.58
  260.4 1.5 fusion.57
  262.0 1.5 add_convert_fusion
  263.5 16.5 %copy.52 = bf16[64,16,1280]{1,0,2:T(8,128)(2,1)} copy(bf16[64,16,1280]{2,1,0:T(8,128)(2,1)S(1)} %bitcast.91) | data formatting | bytes 5242880
  280.0 36.8 %reshape.148 = bf16[1280,1024]{1,0:T(8,128)(2,1)} reshape(bf16[1280,64,16]{2,1,0:T(8,128)(2,1)} %bitcast.88) | data formatting | bytes 5242880
  316.8 1.1 copy-done.22
  317.9 3.1 fusion.5
  321.0 94.2 %fusion = bf16[384,48]{0,1:T(8,128)(2,1)S(1)} fusion(bf16[384,1152]{0,1:T(8,128)(2,1)S(1)} %fusion.5), kind=kCustom, calls=%all-reduce-scatter | all-reduce-scatter fusion | flops 589825 | bytes 922112
  415.2 1.3 collective-permute-start.6
  416.5 1.3 collective-permute-start.5
  417.8 1.3 collective-permute-start.7
  419.1 1.3 collective-permute-start.4
  420.4 7.7 collective-permute-start.3
  428.2 1.3 collective-permute-start.2
  429.5 4.8 collective-permute-start.1
  434.3 3.7 collective-permute-start
  440.0 1.9 concatenate
  442.5 27.3 %reduce-scatter.22.cloned.1.call-done = bf16[384,32]{0,1:T(8,128)(2,1)} async-done(((bf16[384,1024]{0,1:T(8,128)(2,1)}), bf16[384,32]{0,1:T(8,128)(2,1)}) %reduce-scatter.22.cloned.1.call-update) | async-done | bytes 24592 | tf_op jit(solution)/shard_map/reduce_scatter | solution.py:77
  469.8 1.4 convert_element_type.217
  471.2 222.1 %reduce-scatter.20.cloned.1.call-done = bf16[384,48]{0,1:T(8,128)(2,1)} async-done(((bf16[384,1536]{0,1:T(8,128)(2,1)}), bf16[384,48]{0,1:T(8,128)(2,1)}) %reduce-scatter.20.cloned.1.call-update) | async-done | bytes 36880 | tf_op jit(solution)/shard_map/reduce_scatter | solution.py:77
  693.3 1.4 convert_element_type.207
  694.7 348.8 %all-reduce.8.cloned.1.call-done = (bf16[1280,384]{0,1:T(8,128)(2,1)}, bf16[1280,384]{0,1:T(8,128)(2,1)}, bf16[1280,384]{0,1:T(8,128)(2,1)}) async-done(((bf16[1280,384]{0,1:T(8,128)(2,1)}, bf16[1280,384]{0,1:T(8,128)(2,1)}, bf16[1280,384]{0,1:T(8,128)(2,1)}), (bf16[1280,384]{0,1:T(8,128)(2,1)}, bf16[1280,384]{0,1:T(8,128)(2,1)}, bf16[1280,384]{0,1:T(8,128)(2,1)})) %all-reduce.8.cloned.1.call-update) | async-done | bytes 2949136
  1043.5 1.0 dynamic-slice_convert_fusion.2
  1045.2 1.1 dynamic-slice_convert_fusion
  1047.8 47.5 %reduce-scatter.26.cloned.1.call-done = bf16[320,1024]{1,0:T(8,128)(2,1)} async-done(((bf16[1280,1024]{1,0:T(8,128)(2,1)}), bf16[320,1024]{1,0:T(8,128)(2,1)}) %reduce-scatter.26.cloned.1.call-update) | async-done | bytes 655376
  1095.3 6.3 reshape.149
  1101.6 6.8 copy.53
  (98 shorter events, 10.1 us)
Async XLA Ops:
  7.2 1.7 copy-start
  7.2 55.7 %reduce-scatter.18.cloned.1.call-start = ((), (), s32[]{:S(2)}) async-start(), calls=%async_computation.12 | async-start | bytes 2621440 | tf_op jit(solution)/shard_map/reduce_scatter | solution.py:59
  8.9 4.8 copy-start.17
  12.9 0.9 copy-start.19
  16.4 80.7 %reduce-scatter.24.cloned.1.call-start = ((), (), s32[]{:S(2)}) async-start(), calls=%async_computation.16 | async-start | bytes 3932160
  16.5 4.0 copy-start.14
  19.3 1.2 copy-start.23
  28.6 5.0 copy-start.16
  28.6 112.5 %reduce-scatter.16.cloned.1.call-start = ((), (), s32[]{:S(2)}) async-start(), calls=%async_computation.10 | async-start | bytes 2949120 | tf_op jit(solution)/shard_map/reduce_scatter | solution.py:59
  32.7 0.9 copy-start.21
  36.5 0.7 copy-start.11
  36.5 1.0 copy-start.9
  36.5 14.1 %copy-start.10 = (s32[1024]{0:T(1024)S(1)}, s32[1024]{0:T(1024)}, u32[]{:S(2)}) copy-start(s32[1024]{0:T(1024)} %param.17) | copy-start | bytes 12292
  38.9 24.0 %all-to-all-start.2 = ((bf16[32,2,16,256]{3,2,1,0:T(8,128)(2,1)}), bf16[32,2,16,256]{3,2,1,0:T(8,128)(2,1)S(1)}, u32[]{:S(2)}, u32[]{:S(2)}) async-start(bf16[32,2,16,256]{3,2,1,0:T(8,128)(2,1)} %copy.45), calls=%async_computation.4 | async-start | bytes 1048576 | tf_op jit(solution)/shard_map/all_to_all | solution.py:131
  50.3 120.8 %all-gather.8.cloned.1.call-start = ((), (), s32[]{:S(2)}) async-start(), calls=%async_computation.13 | async-start | bytes 2621440 | tf_op jit(solution)/shard_map/all_gather | solution.py:68
  67.5 31.9 %all-to-all-start = ((bf16[32,2,16,384]{3,2,1,0:T(8,128)(2,1)}), bf16[32,2,16,384]{3,2,1,0:T(8,128)(2,1)S(1)}, u32[]{:S(2)}, u32[]{:S(2)}) async-start(bf16[32,2,16,384]{3,2,1,0:T(8,128)(2,1)} %copy.39), calls=%async_computation | async-start | bytes 1572864 | tf_op jit(solution)/shard_map/all_to_all | solution.py:131
  71.4 140.6 %all-gather.4.cloned.1.call-start = ((), (), s32[]{:S(2)}) async-start(), calls=%async_computation.9 | async-start | bytes 3932160 | tf_op jit(solution)/shard_map/all_gather | solution.py:68
  101.7 144.1 %all-gather.6.cloned.1.call-start = ((), (), s32[]{:S(2)}) async-start(), calls=%async_computation.11 | async-start | bytes 2949120 | tf_op jit(solution)/shard_map/all_gather | solution.py:68
  141.2 29.9 %copy-start.20 = (bf16[1024,384]{1,0:T(8,128)(2,1)S(1)}, bf16[1024,384]{1,0:T(8,128)(2,1)}, u32[]{:S(2)}) copy-start(bf16[1024,384]{1,0:T(8,128)(2,1)} %copy-done.19) | copy-start | bytes 2359300
  143.8 326.1 %reduce-scatter.22.cloned.1.call-start = ((), (), s32[]{:S(2)}) async-start(), calls=%async_computation.15 | async-start | bytes 811008 | tf_op jit(solution)/shard_map/reduce_scatter | solution.py:77
  174.9 42.4 %copy-start.18 = (bf16[384,1024]{1,0:T(8,128)(2,1)S(1)}, bf16[384,1024]{1,0:T(8,128)(2,1)}, u32[]{:S(2)}) copy-start(bf16[384,1024]{1,0:T(8,128)(2,1)} %param.23) | copy-start | bytes 2359300
  174.9 518.4 %reduce-scatter.20.cloned.1.call-start = ((), (), s32[]{:S(2)}) async-start(), calls=%async_computation.14 | async-start | bytes 1216512 | tf_op jit(solution)/shard_map/reduce_scatter | solution.py:77
  217.3 826.2 %all-reduce.8.cloned.1.call-start = ((), (), s32[]{:S(2)}) async-start(), calls=%async_computation.18 | async-start | bytes 5898240
  220.9 0.9 copy-start.4
  245.8 6.5 copy-start.24
  250.1 2.2 copy-start.13
  250.1 2.3 copy-start.15
  254.5 0.9 copy-start.2
  257.6 1.2 copy-start.7
  257.6 2.7 copy-start.3
  257.6 837.7 %reduce-scatter.26.cloned.1.call-start = ((), (), s32[]{:S(2)}) async-start(), calls=%async_computation.17 | async-start | bytes 3276800
  258.8 1.6 copy-start.8
  260.4 1.6 copy-start.5
  260.4 1.6 copy-start.6
  316.8 1.1 copy-start.22
  317.9 120.1 %copy-start.12 = (u32[128]{0:T(128)S(1)}, u32[128]{0:T(128)}, u32[]{:S(2)}) copy-start(u32[128]{0:T(128)} %constant.39) | copy-start | bytes 1540
  415.2 14.3 %collective-permute-start.6 = (bf16[384,48]{0,1:T(8,128)(2,1)S(1)}, bf16[384,48]{0,1:T(8,128)(2,1)S(1)}, u32[]{:S(2)}, u32[]{:S(2)}) collective-permute-start(bf16[384,48]{0,1:T(8,128)(2,1)S(1)} %fusion), channel_id=1, source_target_pairs={{0,28},{4,32},{8,36},{12,40},{16,44},{20,48},{24,52},{28,56},{32,6... | collective-permute-start | bytes 110600
  416.5 17.8 %collective-permute-start.5 = (bf16[384,48]{0,1:T(8,128)(2,1)S(1)}, bf16[384,48]{0,1:T(8,128)(2,1)S(1)}, u32[]{:S(2)}, u32[]{:S(2)}) collective-permute-start(bf16[384,48]{0,1:T(8,128)(2,1)S(1)} %fusion), channel_id=1, source_target_pairs={{0,24},{4,28},{8,32},{12,36},{16,40},{20,44},{24,48},{28,52},{32,5... | collective-permute-start | bytes 110600
  417.8 10.3 collective-permute-start.7
  419.1 20.8 %collective-permute-start.4 = (bf16[384,48]{0,1:T(8,128)(2,1)S(1)}, bf16[384,48]{0,1:T(8,128)(2,1)S(1)}, u32[]{:S(2)}, u32[]{:S(2)}) collective-permute-start(bf16[384,48]{0,1:T(8,128)(2,1)S(1)} %fusion), channel_id=1, source_target_pairs={{0,20},{4,24},{8,28},{12,32},{16,36},{20,40},{24,44},{28,48},{32,5... | collective-permute-start | bytes 110600
  420.4 19.5 %collective-permute-start.3 = (bf16[384,48]{0,1:T(8,128)(2,1)S(1)}, bf16[384,48]{0,1:T(8,128)(2,1)S(1)}, u32[]{:S(2)}, u32[]{:S(2)}) collective-permute-start(bf16[384,48]{0,1:T(8,128)(2,1)S(1)} %fusion), channel_id=1, source_target_pairs={{0,16},{4,20},{8,24},{12,28},{16,32},{20,36},{24,40},{28,44},{32,4... | collective-permute-start | bytes 110600
  428.2 11.8 %collective-permute-start.2 = (bf16[384,48]{0,1:T(8,128)(2,1)S(1)}, bf16[384,48]{0,1:T(8,128)(2,1)S(1)}, u32[]{:S(2)}, u32[]{:S(2)}) collective-permute-start(bf16[384,48]{0,1:T(8,128)(2,1)S(1)} %fusion), channel_id=1, source_target_pairs={{0,12},{4,16},{8,20},{12,24},{16,28},{20,32},{24,36},{28,40},{32,4... | collective-permute-start | bytes 110600
  429.5 10.5 collective-permute-start.1
  434.3 5.7 collective-permute-start
  1101.6 6.8 copy-start.1
Sparse Core Ops, SparseCore 0:
  16.5 31.6 reduce-scatter.17
  50.8 46.2 reduce-scatter.23
  99.6 39.7 reduce-scatter.15
  141.0 30.0 all-gather.7
  173.3 38.6 all-gather.3
  213.6 32.1 all-gather.5
  251.3 218.5 reduce-scatter.21
  474.6 218.5 reduce-scatter.19
  696.2 347.2 all-reduce.7
  1045.7 49.5 reduce-scatter.25
where the time goes:
time: 1120 us
  waiting for transfers between devices  768 us (69%)
  blocking collectives  128 us (11%)
  local copies, waits for them, and re-layouts  93 us (8%)
  matrix products  56.2 us (5%)
  starting transfers between devices  38.8 us (3%)
  between operations  16.6 us (1%)
  other arithmetic  15 us (1%)
    unnamed x21, waiting for transfers between devices  422 us
    reduce_scatter x2, waiting for transfers between devices, adapt(): lax.psum_scatter((project_grad * loss_scale).astype(jnp.bfloat16), 'dp',...  249 us
    unnamed x1, blocking collectives  94.2 us
    unnamed x62, local copies, waits for them, and re-layouts  87.1 us
    all_gather x3, waiting for transfers between devices, adapt(): lax.all_gather(residual, 'mp', axis=1, tiled=True)  84.5 us
    all_to_all x1, blocking collectives, shards(): lax.all_to_all(for_sending(outgoing), 'dp', split_axis=0, concat_axis=0,...  33.6 us
    unnamed x11, starting transfers between devices  23 us
  transfers between devices with their start and end apart: 20, of which 9 were waited for; matrix products, arithmetic and copies ran while one was open for 21% of the time, Pallas kernels for 0%

commit v1 on v0

v1 whole, which is shorter than its diff:
```python
import jax
import jax.numpy as jnp
from jax import lax
from jax.sharding import Mesh
from jax.sharding import PartitionSpec as P

DP = ("y", "z", "xh")
MP = ("xl", "core")
SIZES = (4, 4, 2, 2, 2)


def gelu_parts(hidden):
    normal_cdf = 0.5 * (1.0 + jax.scipy.special.erf(hidden * 0.7071067811865476))
    density = jnp.exp(-0.5 * hidden * hidden) * 0.3989422804014327
    return (hidden * normal_cdf, normal_cdf + hidden * density)


def swap(value, axis):
    return lax.ppermute(value, axis, [(0, 1), (1, 0)])


def mm(a, b, dims):
    return lax.dot_general(a, b, (dims, ((), ())), preferred_element_type=jnp.float32)


def row_plan(owners, counts, rows, core, block):
    images, patches = owners.shape[0], 16
    index = jnp.arange(images, dtype=jnp.int32)
    earlier = index[None, :] < index[:, None]
    rank = jnp.sum(((owners[:, None] == owners[None, :]) & earlier).astype(jnp.int32), axis=1)
    start = jnp.sum(jnp.where(earlier, counts[None, :], 0), axis=1)
    patch = jnp.arange(patches, dtype=jnp.int32)
    live = patch[None, :] < counts[:, None]
    number = start[:, None] + patch[None, :]
    quarter = rows // 4
    place = ((number // quarter) ^ block ^ 3) * quarter + number % quarter
    place = jnp.where(live, place, -1).reshape(-1)
    source = ((rank ^ core)[:, None] * 32 + owners[:, None]) * patches + patch[None, :]
    source = jnp.where(live, source, -1).reshape(-1)
    here = place[None, :] == jnp.arange(rows, dtype=jnp.int32)[:, None]
    origin = jnp.sum(jnp.where(here, source[None, :] + 1, 0), axis=1) - 1
    total = 2 * 32 * patches
    from_slots = origin[:, None] == jnp.arange(total, dtype=jnp.int32)[None, :]
    return here.astype(jnp.bfloat16), from_slots.astype(jnp.bfloat16)


def gather_targets(targets, core, xl, quarter):
    sent = [t[: 2 * quarter] for t in targets]
    got = swap(tuple(sent), "core")
    kept = [t[2 * quarter :] for t in targets]
    pairs = [
        jnp.concatenate([jnp.where(core == 0, k, g), jnp.where(core == 0, g, k)], axis=1)
        for k, g in zip(kept, got)
    ]
    far = swap(tuple(p[:quarter] for p in pairs), "xl")
    near = [p[quarter:] for p in pairs]
    return [
        jnp.concatenate([jnp.where(xl == 0, n, f), jnp.where(xl == 0, f, n)], axis=1)
        for n, f in zip(near, far)
    ]


def sum_over_dp(expand_grad, project_grad):
    width = project_grad.shape[0]
    e = expand_grad
    for axis in ("y", "z", "xh"):
        e = lax.psum_scatter(e, axis, scatter_dimension=0, tiled=True)
    p = project_grad.reshape(4, 4, width // 16, -1).transpose(1, 0, 2, 3)
    p = p.reshape(width, -1)
    p = lax.psum_scatter(p, "z", scatter_dimension=0, tiled=True)
    p = lax.psum_scatter(p, "y", scatter_dimension=0, tiled=True)
    p = lax.psum_scatter(p, "xh", scatter_dimension=0, tiled=True)
    return e.astype(jnp.float32), p.astype(jnp.float32).T


def step(student, targets, owners, counts, loss_scale, weights, rows):
    core, xl = lax.axis_index("core"), lax.axis_index("xl")
    block = core * 2 + xl
    quarter = rows // 4
    half = rows // 2
    to_rows, from_slots = row_plan(owners, counts, rows, core, block)

    slots = student.reshape(32, 2, 16, -1)
    mine = lax.dynamic_index_in_dim(slots, core, 1, keepdims=False)
    mine = lax.all_to_all(mine, DP, split_axis=0, concat_axis=0, tiled=True)
    mine = mine.reshape(32 * 16, -1)
    other = swap(mine, "core")
    x = (mm(from_slots[:, :512], mine, ((1,), (0,))) + mm(from_slots[:, 512:], other, ((1,), (0,)))).astype(jnp.bfloat16)

    compact = [
        mm(to_rows, t.reshape(512, -1), ((1,), (0,))).astype(jnp.bfloat16) for t in targets
    ]
    wanted = gather_targets(compact, core, xl, quarter)

    acts, slopes, residuals = [], [], []
    for (expand, project), target in zip(weights, wanted):
        hidden = mm(x, expand, ((1,), (0,)))
        act, slope = gelu_parts(hidden)
        act = act.astype(jnp.bfloat16)
        near = swap(mm(act[:half], project, ((1,), (0,))).astype(jnp.bfloat16), "core")
        far_sum = mm(act[half : half + quarter], project, ((1,), (0,))) + near[:quarter].astype(jnp.float32)
        far = swap(far_sum.astype(jnp.bfloat16), "xl")
        own = mm(act[half + quarter :], project, ((1,), (0,))) + near[quarter:].astype(jnp.float32)
        residual = (own + far.astype(jnp.float32)) - target.astype(jnp.float32)
        acts.append(act)
        slopes.append(slope)
        residuals.append(residual.astype(jnp.bfloat16))

    results, hidden_grads = [], []
    for (expand, project), act, slope, own in zip(weights, acts, slopes, residuals):
        by_core = swap(own, "core")
        by_xl = swap(own, "xl")
        by_both = swap(by_xl, "core")
        residual = jnp.concatenate([by_both, by_core, by_xl, own], axis=0)
        project_grad = (mm(residual, act, ((0,), (0,))) * loss_scale).astype(jnp.bfloat16)
        back = mm(residual, project, ((1,), (1,)))
        hidden_grad = (back * slope).astype(jnp.bfloat16)
        expand_grad = (mm(x, hidden_grad, ((0,), (0,))) * loss_scale).astype(jnp.bfloat16)
        results.extend(sum_over_dp(expand_grad, project_grad))
        hidden_grads.append(hidden_grad)

    def columns(xl_of, core_of):
        start = (xl_of * 2 + core_of) * 320
        total = 0.0
        for (expand, _), hidden_grad in zip(weights, hidden_grads):
            part = lax.dynamic_slice_in_dim(expand, start, 320, 0)
            total = total + mm(hidden_grad, part, ((1,), (1,)))
        return total

    def core_order(value):
        return jnp.concatenate([value[half:], value[:half]], axis=0)

    def xl_order(value):
        cuts = [value[i * quarter : (i + 1) * quarter] for i in range(4)]
        return jnp.concatenate([cuts[1], cuts[0], cuts[3], cuts[2]], axis=0)

    near_far = swap(columns(1 - xl, 1 - core).astype(jnp.bfloat16), "core")
    near_own = swap(columns(xl, 1 - core).astype(jnp.bfloat16), "core")
    far = swap(
        (columns(1 - xl, core) + core_order(near_far).astype(jnp.float32)).astype(jnp.bfloat16), "xl"
    )
    own = columns(xl, core) + core_order(near_own).astype(jnp.float32)
    grad = (own + xl_order(far).astype(jnp.float32)).astype(jnp.bfloat16)
    placed = mm(from_slots, grad, ((0,), (0,))).astype(jnp.bfloat16).reshape(2, 32, 16, -1)
    placed = jnp.where(core == 0, placed, placed[::-1]).transpose(1, 0, 2, 3)
    sent = lax.all_to_all(placed, DP, split_axis=0, concat_axis=0, tiled=True)
    return (sent.reshape(student.shape[0], 16, -1), *results)


def shards(
    student,
    dino_target,
    siglip_target,
    clip_target,
    image_owner,
    patch_count,
    dino_expand,
    dino_project,
    siglip_expand,
    siglip_project,
    clip_expand,
    clip_project,
):
    store = (lax.axis_index("y") * 4 + lax.axis_index("z")) * 2 + lax.axis_index("xh")
    per_store = dino_target.shape[0]
    owners = lax.dynamic_slice_in_dim(image_owner[:, 0], store * per_store, per_store)
    counts = lax.dynamic_slice_in_dim(patch_count, store * per_store, per_store)
    loss_scale = 1.0 / jnp.sqrt(jnp.sum(patch_count).astype(jnp.float32))
    weights = (
        (dino_expand, dino_project),
        (siglip_expand, siglip_project),
        (clip_expand, clip_project),
    )
    return step(
        student, (dino_target, siglip_target, clip_target), owners, counts, loss_scale, weights, 512
    )


def solution(mesh):
    fine = Mesh(mesh.devices.reshape(SIZES), DP + MP)
    return jax.shard_map(
        shards,
        mesh=fine,
        in_specs=(
            P(DP, None, None),
            P(DP, None, MP),
            P(DP, None, MP),
            P(DP, None, MP),
            P(),
            P(),
            P(None, MP),
            P(MP, None),
            P(None, MP),
            P(MP, None),
            P(None, MP),
            P(MP, None),
        ),
        out_specs=(
            P(DP, None, MP),
            P(DP, MP),
            P(MP, DP),
            P(DP, MP),
            P(MP, DP),
            P(DP, MP),
            P(MP, DP),
        ),
        check_vma=False,
    )
```

time: 1120 us -> 456 us (0.41)
  waiting for transfers between devices: 768 us -> 286 us
  blocking collectives: 128 us -> 9.13 us
  local copies, waits for them, and re-layouts: 93 us -> 19.3 us
    unnamed x21 -> x22, waiting for transfers between devices: 422 us -> 63 us
    unnamed x1, blocking collectives: 94.2 us -> 9.13 us
    all_gather x3 -> x0, waiting for transfers between devices: 84.5 us -> none  [adapt(): lax.all_gather(residual, 'mp', axis=1, tiled=True)]
    unnamed x62 -> x110, local copies, waits for them, and re-layouts: 87.1 us -> 5.63 us
    reduce_scatter x4 -> x13, waiting for transfers between devices: 249 us -> 172 us  [the longest x6 74.6 us: sum_over_dp(): e = lax.psum_scatter(e, axis, scatter_dimension=0, tiled=True)]
    ppermute x0 -> x25, waiting for transfers between devices: none -> 39.4 us  [swap(): return lax.ppermute(value, axis, [(0, 1), (1, 0)])]
    all_to_all x1 -> x0, blocking collectives: 33.6 us -> none  [shards(): lax.all_to_all(for_sending(outgoing), 'dp', split_axis=0, concat_axis=0,...]
    unnamed x11 -> x5, starting transfers between devices: 23 us -> 2.34 us
  transfers between devices with their start and end apart: 20 -> 45, of which waited for: 9 -> 22; matrix products, arithmetic and copies ran while one was open for 21% -> 23% of each run, Pallas kernels for 0% -> 0%
where the time goes in v1:
time: 456 us; the launch traced here: 454 us
  waiting for transfers between devices  286 us (63%)
  matrix products  62.4 us (14%)
  starting transfers between devices  42.2 us (9%)
  other arithmetic  19.5 us (4%)
  local copies, waits for them, and re-layouts  19.3 us (4%)
  between operations  16.2 us (4%)
  blocking collectives  9.13 us (2%)
    reduce_scatter x6, waiting for transfers between devices, sum_over_dp(): e = lax.psum_scatter(e, axis, scatter_dimension=0, tiled=True)  74.6 us
    unnamed x22, waiting for transfers between devices  63 us
    dot_general x38, matrix products, mm(): lax.dot_general(a, b, (dims, ((), ())), preferred_element_type=jnp.float32)  62.4 us
    reduce_scatter x3, waiting for transfers between devices, sum_over_dp(): p = lax.psum_scatter(p, 'z', scatter_dimension=0, tiled=True)  43.5 us
    ppermute x25, waiting for transfers between devices, swap(): return lax.ppermute(value, axis, [(0, 1), (1, 0)])  39.4 us
    reduce_scatter x2, waiting for transfers between devices, sum_over_dp(): p = lax.psum_scatter(p, 'xh', scatter_dimension=0, tiled=True)  32 us
    reduce_scatter x2, waiting for transfers between devices, sum_over_dp(): p = lax.psum_scatter(p, 'y', scatter_dimension=0, tiled=True)  21.5 us
    ppermute x25, starting transfers between devices, swap(): return lax.ppermute(value, axis, [(0, 1), (1, 0)])  19.9 us
  transfers between devices with their start and end apart: 45, of which 22 were waited for; matrix products, arithmetic and copies ran while one was open for 23% of the time, Pallas kernels for 0%

profile of v1, /device:TPU:1, one launch (start us, length us, event | category | flops | bytes accessed | tf_op | source)
XLA Modules:
  0.0 454.4 jit_solution(7968062518804463606)
XLA Ops:
  7.2 1.7 copy-done
  10.1 11.6 %all-to-all-start = ((bf16[32,16,1280]{2,1,0:T(8,128)(2,1)}), bf16[32,16,1280]{2,1,0:T(8,128)(2,1)}, u32[]{:S(2)}, u32[]{:S(2)}) async-start(bf16[32,16,1280]{2,1,0:T(8,128)(2,1)} %dynamic-slice_bitcast_fusion), calls=%async_computation | async-start | bytes 2621440 | tf_op jit(solution)/shard_map/all_to_all | solution.py:85
  26.1 1.4 convolution_convert_fusion.4
  28.2 1.4 convolution_convert_fusion.5
  31.1 11.5 %all-to-all-done = bf16[32,16,1280]{2,1,0:T(8,128)(2,1)} async-done(((bf16[32,16,1280]{2,1,0:T(8,128)(2,1)}), bf16[32,16,1280]{2,1,0:T(8,128)(2,1)}, u32[]{:S(2)}, u32[]{:S(2)}) %all-to-all-start) | async-done | bytes 1310752 | tf_op jit(solution)/shard_map/all_to_all | solution.py:85
  42.6 2.2 collective-permute-start
  50.1 2.2 fusion.13
  52.4 2.3 fusion.1
  54.8 1.7 multiply_convert_fusion.1
  62.5 9.2 %collective-permute-done.16 = bf16[128,1024]{1,0:T(8,128)(2,1)S(1)} collective-permute-done((bf16[128,1024]{1,0:T(8,128)(2,1)S(1)}, bf16[128,1024]{1,0:T(8,128)(2,1)S(1)}, u32[]{:S(2)}, u32[]{:S(2)}) %collective-permute-start.16) | collective-permute-done | bytes 262176 | tf_op jit(solution)/shard_map/ppermute | solution.py:19
  72.2 1.7 multiply_convert_fusion.2
  75.1 3.9 collective-permute-done.19
  79.0 1.7 collective-permute-start.20
  84.1 3.4 multiply_convert_fusion.3
  87.5 1.5 convolution_convert_fusion
  90.8 2.0 add_convert_fusion.3
  94.8 1.8 fusion.5
  96.8 5.0 %collective-permute-done.9 = bf16[128,1152]{1,0:T(8,128)(2,1)} collective-permute-done((bf16[128,1152]{1,0:T(8,128)(2,1)}, bf16[128,1152]{1,0:T(8,128)(2,1)}, u32[]{:S(2)}, u32[]{:S(2)}) %collective-permute-start.9) | collective-permute-done | bytes 294944 | tf_op jit(solution)/shard_map/ppermute | solution.py:19
  101.8 1.5 subtract_convert_fusion.1
  103.7 1.7 broadcast_select_fusion.5
  106.5 4.6 %collective-permute-done.12 = bf16[128,1152]{1,0:T(8,128)(2,1)S(1)} collective-permute-done((bf16[128,1152]{1,0:T(8,128)(2,1)S(1)}, bf16[128,1152]{1,0:T(8,128)(2,1)S(1)}, u32[]{:S(2)}, u32[]{:S(2)}) %collective-permute-start.12) | collective-permute-done | bytes 294944 | tf_op jit(solution)/shard_map/ppermute | solution.py:19
  111.1 1.7 collective-permute-start.13
  114.0 2.1 add_convert_fusion
  118.3 1.8 fusion.4
  120.2 7.0 %collective-permute-done.2 = bf16[128,1536]{1,0:T(8,128)(2,1)} collective-permute-done((bf16[128,1536]{1,0:T(8,128)(2,1)}, bf16[128,1536]{1,0:T(8,128)(2,1)}, u32[]{:S(2)}, u32[]{:S(2)}) %collective-permute-start.2) | collective-permute-done | bytes 393248 | tf_op jit(solution)/shard_map/ppermute | solution.py:19
  127.2 1.4 subtract_convert_fusion
  130.1 8.4 %collective-permute-done.5 = bf16[128,1536]{1,0:T(8,128)(2,1)S(1)} collective-permute-done((bf16[128,1536]{1,0:T(8,128)(2,1)S(1)}, bf16[128,1536]{1,0:T(8,128)(2,1)S(1)}, u32[]{:S(2)}, u32[]{:S(2)}) %collective-permute-start.5) | collective-permute-done | bytes 393248 | tf_op jit(solution)/shard_map/ppermute | solution.py:19
  138.5 1.7 collective-permute-start.6
  143.1 1.8 fusion.3
  145.0 2.1 fusion.6
  148.2 2.4 fusion.2
  151.8 1.4 fusion.43
  154.5 2.0 fusion.11
  158.3 2.1 convolution_add_fusion.4
  161.8 2.2 convolution_add_fusion.6
  164.1 2.4 fusion.10
  166.7 2.1 fusion.58
  169.9 6.2 %reduce-scatter.28.cloned.1.call-done = bf16[320,384]{1,0:T(8,128)(2,1)} async-done(((bf16[1280,384]{1,0:T(8,128)(2,1)}), bf16[320,384]{1,0:T(8,128)(2,1)}) %reduce-scatter.28.cloned.1.call-update) | async-done | bytes 245776 | tf_op jit(solution)/shard_map/reduce_scatter | solution.py:67
  176.2 2.5 add_convert_fusion.2
  179.8 2.1 convolution_add_fusion.8
  181.9 19.7 %reduce-scatter.42.cloned.1.call-done = bf16[288,384]{1,0:T(8,128)(2,1)} async-done(((bf16[1152,384]{1,0:T(8,128)(2,1)}), bf16[288,384]{1,0:T(8,128)(2,1)}) %reduce-scatter.42.cloned.1.call-update) | async-done | bytes 221200 | tf_op jit(solution)/shard_map/reduce_scatter | solution.py:70
  202.8 1.7 fusion.115
  204.5 23.8 %reduce-scatter.32.cloned.1.call-done = bf16[384,384]{1,0:T(8,128)(2,1)} async-done(((bf16[1536,384]{1,0:T(8,128)(2,1)}), bf16[384,384]{1,0:T(8,128)(2,1)}) %reduce-scatter.32.cloned.1.call-update) | async-done | bytes 294928 | tf_op jit(solution)/shard_map/reduce_scatter | solution.py:70
  228.3 2.9 convolution_convert_fusion.2
  231.2 1.4 copy.52
  233.7 7.8 %all-to-all-start.1 = ((bf16[32,2,16,320]{3,2,1,0:T(8,128)(2,1)}), bf16[32,2,16,320]{3,2,1,0:T(8,128)(2,1)S(1)}, u32[]{:S(2)}, u32[]{:S(2)}) async-start(bf16[32,2,16,320]{3,2,1,0:T(8,128)(2,1)} %copy.53), calls=%async_computation.1 | async-start | bytes 1572864 | tf_op jit(solution)/shard_map/all_to_all | solution.py:146
  241.6 10.0 %reduce-scatter.50.cloned.1.call-done = bf16[64,384]{1,0:T(8,128)(2,1)} async-done(((bf16[256,384]{1,0:T(8,128)(2,1)}), bf16[64,384]{1,0:T(8,128)(2,1)}) %reduce-scatter.50.cloned.1.call-update) | async-done | bytes 49168 | tf_op jit(solution)/shard_map/reduce_scatter | solution.py:71
  251.6 22.8 %reduce-scatter.46.cloned.1.call-done = bf16[80,384]{1,0:T(8,128)(2,1)} async-done(((bf16[320,384]{1,0:T(8,128)(2,1)}), bf16[80,384]{1,0:T(8,128)(2,1)}) %reduce-scatter.46.cloned.1.call-update) | async-done | bytes 61456 | tf_op jit(solution)/shard_map/reduce_scatter | solution.py:67
  274.5 22.9 %reduce-scatter.40.cloned.1.call-done = bf16[80,384]{1,0:T(8,128)(2,1)} async-done(((bf16[320,384]{1,0:T(8,128)(2,1)}), bf16[80,384]{1,0:T(8,128)(2,1)}) %reduce-scatter.40.cloned.1.call-update) | async-done | bytes 61456 | tf_op jit(solution)/shard_map/reduce_scatter | solution.py:67
  297.5 22.6 %reduce-scatter.30.cloned.1.call-done = bf16[80,384]{1,0:T(8,128)(2,1)} async-done(((bf16[320,384]{1,0:T(8,128)(2,1)}), bf16[80,384]{1,0:T(8,128)(2,1)}) %reduce-scatter.30.cloned.1.call-update) | async-done | bytes 61456 | tf_op jit(solution)/shard_map/reduce_scatter | solution.py:67
  321.5 21.3 %reduce-scatter.58.cloned.1.call-done = bf16[72,384]{1,0:T(8,128)(2,1)} async-done(((bf16[288,384]{1,0:T(8,128)(2,1)}), bf16[72,384]{1,0:T(8,128)(2,1)}) %reduce-scatter.58.cloned.1.call-update) | async-done | bytes 55312
  342.8 9.1 %fusion = bf16[48,384]{1,0:T(8,128)(2,1)S(1)} fusion(bf16[72,384]{1,0:T(8,128)(2,1)} %reduce-scatter.58.cloned.1.call-done), kind=kCustom, calls=%all-reduce-scatter | all-reduce-scatter fusion | flops 36865 | bytes 92672
  351.9 2.2 collective-permute-start.25
  354.1 11.5 %reduce-scatter.34.cloned.1.call-done = bf16[96,384]{1,0:T(8,128)(2,1)} async-done(((bf16[384,384]{1,0:T(8,128)(2,1)}), bf16[96,384]{1,0:T(8,128)(2,1)}) %reduce-scatter.34.cloned.1.call-update) | async-done | bytes 73744 | tf_op jit(solution)/shard_map/reduce_scatter | solution.py:71
  365.6 17.8 %reduce-scatter.52.cloned.1.call-done = bf16[32,384]{1,0:T(8,128)(2,1)} async-done(((bf16[64,384]{1,0:T(8,128)(2,1)}), bf16[32,384]{1,0:T(8,128)(2,1)}) %reduce-scatter.52.cloned.1.call-update) | async-done | bytes 24592 | tf_op jit(solution)/shard_map/reduce_scatter | solution.py:72
  383.4 1.4 convert_bitcast_fusion.2
  385.7 13.2 %reduce-scatter.60.cloned.1.call-done = bf16[40,384]{1,0:T(8,128)(2,1)} async-done(((bf16[80,384]{1,0:T(8,128)(2,1)}), bf16[40,384]{1,0:T(8,128)(2,1)}) %reduce-scatter.60.cloned.1.call-update) | async-done | bytes 30736
  398.9 1.4 convert_element_type.203
  400.3 14.1 %reduce-scatter.56.cloned.1.call-done = bf16[40,384]{1,0:T(8,128)(2,1)} async-done(((bf16[80,384]{1,0:T(8,128)(2,1)}), bf16[40,384]{1,0:T(8,128)(2,1)}) %reduce-scatter.56.cloned.1.call-update) | async-done | bytes 30736
  414.4 1.4 convert_element_type.200
  415.8 14.1 %reduce-scatter.54.cloned.1.call-done = bf16[40,384]{1,0:T(8,128)(2,1)} async-done(((bf16[80,384]{1,0:T(8,128)(2,1)}), bf16[40,384]{1,0:T(8,128)(2,1)}) %reduce-scatter.54.cloned.1.call-update) | async-done | bytes 30736
  429.9 1.4 convert_element_type.197
  431.3 14.3 %reduce-scatter.36.cloned.1.call-done = bf16[48,384]{1,0:T(8,128)(2,1)} async-done(((bf16[96,384]{1,0:T(8,128)(2,1)}), bf16[48,384]{1,0:T(8,128)(2,1)}) %reduce-scatter.36.cloned.1.call-update) | async-done | bytes 36880 | tf_op jit(solution)/shard_map/reduce_scatter | solution.py:72
  445.5 1.4 convert_bitcast_fusion
  (239 shorter events, 50.3 us)
Async XLA Ops:
  10.1 11.7 %copy-start.35 = (s32[1024]{0:T(1024)S(1)}, s32[1024]{0:T(1024)}, u32[]{:S(2)}) copy-start(s32[1024]{0:T(1024)} %param.17) | copy-start | bytes 12292
  10.1 14.0 %copy-start.43 = (bf16[32,16,256]{2,1,0:T(8,128)(2,1)S(1)}, bf16[32,16,256]{2,1,0:T(8,128)(2,1)}, u32[]{:S(2)}) copy-start(bf16[32,16,256]{2,1,0:T(8,128)(2,1)} %param.15) | copy-start | bytes 786436
  10.1 32.5 %all-to-all-start = ((bf16[32,16,1280]{2,1,0:T(8,128)(2,1)}), bf16[32,16,1280]{2,1,0:T(8,128)(2,1)}, u32[]{:S(2)}, u32[]{:S(2)}) async-start(bf16[32,16,1280]{2,1,0:T(8,128)(2,1)} %dynamic-slice_bitcast_fusion), calls=%async_computation | async-start | bytes 2621440 | tf_op jit(solution)/shard_map/all_to_all | solution.py:85
  21.7 135.3 %reduce-scatter.48.cloned.1.call-start = ((), (), s32[]{:S(2)}) async-start(), calls=%async_computation.29 | async-start | bytes 983040 | tf_op jit(solution)/shard_map/reduce_scatter | solution.py:70
  25.1 21.3 %collective-permute-start.17 = (bf16[256,256]{1,0:T(8,128)(2,1)}, bf16[256,256]{1,0:T(8,128)(2,1)S(1)}, u32[]{:S(2)}, u32[]{:S(2)}) collective-permute-start(bf16[256,256]{1,0:T(8,128)(2,1)} %slice.174), channel_id=1, source_target_pairs={{0,1},{1,0},{2,3},{3,2},{4,5},{5,4},{6,7},{7,6},{8,9},{9,8},{10,11... | collective-permute-start | bytes 393224 | tf_op jit(solution)/shard_map/ppermute | solution.py:19
  28.2 19.6 %collective-permute-start.10 = (bf16[256,288]{1,0:T(8,128)(2,1)}, bf16[256,288]{1,0:T(8,128)(2,1)}, u32[]{:S(2)}, u32[]{:S(2)}) collective-permute-start(bf16[256,288]{1,0:T(8,128)(2,1)} %slice.165), channel_id=1, source_target_pairs={{0,1},{1,0},{2,3},{3,2},{4,5},{5,4},{6,7},{7,6},{8,9},{9,8},{10,11... | collective-permute-start | bytes 442376 | tf_op jit(solution)/shard_map/ppermute | solution.py:19
  30.4 27.2 %collective-permute-start.3 = (bf16[256,384]{1,0:T(8,128)(2,1)}, bf16[256,384]{1,0:T(8,128)(2,1)}, u32[]{:S(2)}, u32[]{:S(2)}) collective-permute-start(bf16[256,384]{1,0:T(8,128)(2,1)} %slice.156), channel_id=1, source_target_pairs={{0,1},{1,0},{2,3},{3,2},{4,5},{5,4},{6,7},{7,6},{8,9},{9,8},{10,11... | collective-permute-start | bytes 589832 | tf_op jit(solution)/shard_map/ppermute | solution.py:19
  42.6 9.8 %collective-permute-start = (bf16[512,1280]{1,0:T(8,128)(2,1)}, bf16[512,1280]{1,0:T(8,128)(2,1)}, u32[]{:S(2)}, u32[]{:S(2)}) collective-permute-start(bf16[512,1280]{1,0:T(8,128)(2,1)} %bitcast.5), channel_id=1, source_target_pairs={{0,1},{1,0},{2,3},{3,2},{4,5},{5,4},{6,7},{7,6},{8,9},{9,8},{10,11... | collective-permute-start | bytes 3932168 | tf_op jit(solution)/shard_map/ppermute | solution.py:19
  47.4 12.3 %collective-permute-start.18 = (bf16[128,512]{1,0:T(8,128)(2,1)S(1)}, bf16[128,512]{1,0:T(8,128)(2,1)S(1)}, u32[]{:S(2)}, u32[]{:S(2)}) collective-permute-start(bf16[128,512]{1,0:T(8,128)(2,1)S(1)} %pad_maximum_fusion.11), channel_id=1, source_target_pairs={{0,2},{2,0},{1,3},{3,1},{4,6},{6,4},{5,7},{7,5},{8,10},{10,8},{9,1... | collective-permute-start | bytes 393224 | tf_op jit(solution)/shard_map/ppermute | solution.py:19
  48.9 12.4 %collective-permute-start.11 = (bf16[128,576]{1,0:T(8,128)(2,1)S(1)}, bf16[128,576]{1,0:T(8,128)(2,1)S(1)}, u32[]{:S(2)}, u32[]{:S(2)}) collective-permute-start(bf16[128,576]{1,0:T(8,128)(2,1)S(1)} %pad_maximum_fusion.10), channel_id=1, source_target_pairs={{0,2},{2,0},{1,3},{3,1},{4,6},{6,4},{5,7},{7,5},{8,10},{10,8},{9,1... | collective-permute-start | bytes 442376 | tf_op jit(solution)/shard_map/ppermute | solution.py:19
  54.8 17.5 %copy-start.18 = (bf16[512,1280]{1,0:T(8,128)(2,1)}, bf16[512,1280]{1,0:T(8,128)(2,1)S(1)}, u32[]{:S(2)}) copy-start(bf16[512,1280]{1,0:T(8,128)(2,1)S(1)} %fusion.1) | copy-start | bytes 3932164
  57.0 2.8 collective-permute-start.15
  59.4 44.3 %collective-permute-start.4 = (bf16[128,768]{1,0:T(8,128)(2,1)}, bf16[128,768]{1,0:T(8,128)(2,1)}, u32[]{:S(2)}, u32[]{:S(2)}) collective-permute-start(bf16[128,768]{1,0:T(8,128)(2,1)} %pad_maximum_fusion.7), channel_id=1, source_target_pairs={{0,2},{2,0},{1,3},{3,1},{4,6},{6,4},{5,7},{7,5},{8,10},{10,8},{9,1... | collective-permute-start | bytes 589832 | tf_op jit(solution)/shard_map/ppermute | solution.py:19
  60.1 11.6 %collective-permute-start.16 = (bf16[128,1024]{1,0:T(8,128)(2,1)S(1)}, bf16[128,1024]{1,0:T(8,128)(2,1)S(1)}, u32[]{:S(2)}, u32[]{:S(2)}) collective-permute-start(bf16[128,1024]{1,0:T(8,128)(2,1)S(1)} %add_convert_fusion.4), channel_id=1, source_target_pairs={{0,2},{2,0},{1,3},{3,1},{4,6},{6,4},{5,7},{7,5},{8,10},{10,8},{9,1... | collective-permute-start | bytes 786440 | tf_op jit(solution)/shard_map/ppermute | solution.py:19
  62.2 10.1 %copy-start.22 = (bf16[1280,384]{1,0:T(8,128)(2,1)S(1)}, bf16[1280,384]{1,0:T(8,128)(2,1)}, u32[]{:S(2)}) copy-start(bf16[1280,384]{1,0:T(8,128)(2,1)} %param.20) | copy-start | bytes 2949124
  71.8 10.2 %copy-start.33 = (bf16[128,1024]{1,0:T(8,128)(2,1)}, bf16[128,1024]{1,0:T(8,128)(2,1)S(1)}, u32[]{:S(2)}) copy-start(bf16[128,1024]{1,0:T(8,128)(2,1)S(1)} %subtract_convert_fusion.2) | copy-start | bytes 786436
  71.8 8.8 %copy-start.4 = (bf16[384,1152]{1,0:T(8,128)(2,1)S(1)}, bf16[384,1152]{1,0:T(8,128)(2,1)}, u32[]{:S(2)}) copy-start(bf16[384,1152]{1,0:T(8,128)(2,1)} %param.21) | copy-start | bytes 2654212
  71.9 7.1 %collective-permute-start.19 = (bf16[128,1024]{1,0:T(8,128)(2,1)S(1)}, bf16[128,1024]{1,0:T(8,128)(2,1)S(1)}, u32[]{:S(2)}, u32[]{:S(2)}) collective-permute-start(bf16[128,1024]{1,0:T(8,128)(2,1)S(1)} %subtract_convert_fusion.2), channel_id=1, source_target_pairs={{0,2},{2,0},{1,3},{3,1},{4,6},{6,4},{5,7},{7,5},{8,10},{10,8},{9,1... | collective-permute-start | bytes 786440 | tf_op jit(solution)/shard_map/ppermute | solution.py:19
  74.0 8.0 %copy-start.27 = (bf16[512,384]{1,0:T(8,128)(2,1)}, bf16[512,384]{1,0:T(8,128)(2,1)S(1)}, u32[]{:S(2)}) copy-start(bf16[512,384]{1,0:T(8,128)(2,1)S(1)} %get-tuple-element.31) | copy-start | bytes 1179652
  74.0 8.0 %collective-permute-start.21 = (bf16[128,1024]{1,0:T(8,128)(2,1)S(1)}, bf16[128,1024]{1,0:T(8,128)(2,1)S(1)}, u32[]{:S(2)}, u32[]{:S(2)}) collective-permute-start(bf16[128,1024]{1,0:T(8,128)(2,1)S(1)} %subtract_convert_fusion.2), channel_id=1, source_target_pairs={{0,1},{1,0},{2,3},{3,2},{4,5},{5,4},{6,7},{7,6},{8,9},{9,8},{10,11... | collective-permute-start | bytes 786440 | tf_op jit(solution)/shard_map/ppermute | solution.py:19
  79.0 3.1 collective-permute-start.20
  82.0 8.8 %collective-permute-start.8 = (bf16[256,1152]{1,0:T(8,128)(2,1)}, bf16[256,1152]{1,0:T(8,128)(2,1)}, u32[]{:S(2)}, u32[]{:S(2)}) collective-permute-start(bf16[256,1152]{1,0:T(8,128)(2,1)} %convolution_convert_fusion.1), channel_id=1, source_target_pairs={{0,1},{1,0},{2,3},{3,2},{4,5},{5,4},{6,7},{7,6},{8,9},{9,8},{10,11... | collective-permute-start | bytes 1769480 | tf_op jit(solution)/shard_map/ppermute | solution.py:19
  83.9 76.6 %reduce-scatter.44.cloned.1.call-start = ((), (), s32[]{:S(2)}) async-start(), calls=%async_computation.27 | async-start | bytes 1228800 | tf_op jit(solution)/shard_map/reduce_scatter | solution.py:67
  89.0 25.0 %collective-permute-start.1 = (bf16[256,1536]{1,0:T(8,128)(2,1)}, bf16[256,1536]{1,0:T(8,128)(2,1)}, u32[]{:S(2)}, u32[]{:S(2)}) collective-permute-start(bf16[256,1536]{1,0:T(8,128)(2,1)} %convolution_convert_fusion), channel_id=1, source_target_pairs={{0,1},{1,0},{2,3},{3,2},{4,5},{5,4},{6,7},{7,6},{8,9},{9,8},{10,11... | collective-permute-start | bytes 2359304 | tf_op jit(solution)/shard_map/ppermute | solution.py:19
  92.8 8.9 %collective-permute-start.9 = (bf16[128,1152]{1,0:T(8,128)(2,1)}, bf16[128,1152]{1,0:T(8,128)(2,1)}, u32[]{:S(2)}, u32[]{:S(2)}) collective-permute-start(bf16[128,1152]{1,0:T(8,128)(2,1)} %add_convert_fusion.3), channel_id=1, source_target_pairs={{0,2},{2,0},{1,3},{3,1},{4,6},{6,4},{5,7},{7,5},{8,10},{10,8},{9,1... | collective-permute-start | bytes 884744 | tf_op jit(solution)/shard_map/ppermute | solution.py:19
  96.7 67.3 %reduce-scatter.38.cloned.1.call-start = ((), (), s32[]{:S(2)}) async-start(), calls=%async_computation.24 | async-start | bytes 1228800 | tf_op jit(solution)/shard_map/reduce_scatter | solution.py:67
  96.7 6.9 %copy-start.15 = (bf16[256,384]{1,0:T(8,128)(2,1)S(1)}, bf16[256,384]{1,0:T(8,128)(2,1)}, u32[]{:S(2)}) copy-start(bf16[256,384]{1,0:T(8,128)(2,1)} %copy-done.14) | copy-start | bytes 589828
  96.8 6.9 %copy-start.17 = (bf16[256,384]{1,0:T(8,128)(2,1)S(1)}, bf16[256,384]{1,0:T(8,128)(2,1)}, u32[]{:S(2)}) copy-start(bf16[256,384]{1,0:T(8,128)(2,1)} %copy-done.16) | copy-start | bytes 589828
  96.8 16.0 %copy-start.2 = (bf16[384,1536]{1,0:T(8,128)(2,1)S(1)}, bf16[384,1536]{1,0:T(8,128)(2,1)}, u32[]{:S(2)}) copy-start(bf16[384,1536]{1,0:T(8,128)(2,1)} %param.19) | copy-start | bytes 3538948
  96.8 16.0 %copy-start.25 = (bf16[512,384]{1,0:T(8,128)(2,1)S(1)}, bf16[512,384]{1,0:T(8,128)(2,1)}, u32[]{:S(2)}) copy-start(bf16[512,384]{1,0:T(8,128)(2,1)} %copy-done.24) | copy-start | bytes 1179652
  103.3 13.2 %copy-start.31 = (bf16[128,1152]{1,0:T(8,128)(2,1)}, bf16[128,1152]{1,0:T(8,128)(2,1)S(1)}, u32[]{:S(2)}) copy-start(bf16[128,1152]{1,0:T(8,128)(2,1)S(1)} %subtract_convert_fusion.1) | copy-start | bytes 884740
  103.3 7.8 %collective-permute-start.12 = (bf16[128,1152]{1,0:T(8,128)(2,1)S(1)}, bf16[128,1152]{1,0:T(8,128)(2,1)S(1)}, u32[]{:S(2)}, u32[]{:S(2)}) collective-permute-start(bf16[128,1152]{1,0:T(8,128)(2,1)S(1)} %subtract_convert_fusion.1), channel_id=1, source_target_pairs={{0,2},{2,0},{1,3},{3,1},{4,6},{6,4},{5,7},{7,5},{8,10},{10,8},{9,1... | collective-permute-start | bytes 884744 | tf_op jit(solution)/shard_map/ppermute | solution.py:19
  105.4 11.1 %copy-start.51 = (f32[512,384]{1,0:T(8,128)S(1)}, f32[512,384]{1,0:T(8,128)}, u32[]{:S(2)}) copy-start(f32[512,384]{1,0:T(8,128)} %get-tuple-element.32) | copy-start | bytes 2359300
  105.4 11.1 %collective-permute-start.14 = (bf16[128,1152]{1,0:T(8,128)(2,1)S(1)}, bf16[128,1152]{1,0:T(8,128)(2,1)S(1)}, u32[]{:S(2)}, u32[]{:S(2)}) collective-permute-start(bf16[128,1152]{1,0:T(8,128)(2,1)S(1)} %subtract_convert_fusion.1), channel_id=1, source_target_pairs={{0,1},{1,0},{2,3},{3,2},{4,5},{5,4},{6,7},{7,6},{8,9},{9,8},{10,11... | collective-permute-start | bytes 884744 | tf_op jit(solution)/shard_map/ppermute | solution.py:19
  111.1 5.4 %collective-permute-start.13 = (bf16[128,1152]{1,0:T(8,128)(2,1)S(1)}, bf16[128,1152]{1,0:T(8,128)(2,1)S(1)}, u32[]{:S(2)}, u32[]{:S(2)}) collective-permute-start(bf16[128,1152]{1,0:T(8,128)(2,1)S(1)} %collective-permute-done.12), channel_id=1, source_target_pairs={{0,1},{1,0},{2,3},{3,2},{4,5},{5,4},{6,7},{7,6},{8,9},{9,8},{10,11... | collective-permute-start | bytes 884744 | tf_op jit(solution)/shard_map/ppermute | solution.py:19
  116.2 11.1 %collective-permute-start.2 = (bf16[128,1536]{1,0:T(8,128)(2,1)}, bf16[128,1536]{1,0:T(8,128)(2,1)}, u32[]{:S(2)}, u32[]{:S(2)}) collective-permute-start(bf16[128,1536]{1,0:T(8,128)(2,1)} %add_convert_fusion), channel_id=1, source_target_pairs={{0,2},{2,0},{1,3},{3,1},{4,6},{6,4},{5,7},{7,5},{8,10},{10,8},{9,1... | collective-permute-start | bytes 1179656 | tf_op jit(solution)/shard_map/ppermute | solution.py:19
  118.3 8.9 %copy-start.12 = (f32[128,1536]{1,0:T(8,128)S(1)}, f32[128,1536]{1,0:T(8,128)}, u32[]{:S(2)}) copy-start(f32[128,1536]{1,0:T(8,128)} %fusion.82) | copy-start | bytes 2359300
  120.2 55.9 %reduce-scatter.28.cloned.1.call-start = ((), (), s32[]{:S(2)}) async-start(), calls=%async_computation.19 | async-start | bytes 1228800 | tf_op jit(solution)/shard_map/reduce_scatter | solution.py:67
  120.2 21.4 %copy-start.3 = (bf16[384,1536]{1,0:T(8,128)(2,1)S(1)}, bf16[384,1536]{1,0:T(8,128)(2,1)}, u32[]{:S(2)}) copy-start(bf16[384,1536]{1,0:T(8,128)(2,1)} %param.19) | copy-start | bytes 3538948
  120.2 21.4 %copy-start.50 = (f32[512,384]{1,0:T(8,128)S(1)}, f32[512,384]{1,0:T(8,128)}, u32[]{:S(2)}) copy-start(f32[512,384]{1,0:T(8,128)} %get-tuple-element.30) | copy-start | bytes 2359300
  128.6 14.1 %copy-start.30 = (bf16[128,1536]{1,0:T(8,128)(2,1)}, bf16[128,1536]{1,0:T(8,128)(2,1)S(1)}, u32[]{:S(2)}) copy-start(bf16[128,1536]{1,0:T(8,128)(2,1)S(1)} %subtract_convert_fusion) | copy-start | bytes 1179652
  128.6 9.9 %collective-permute-start.5 = (bf16[128,1536]{1,0:T(8,128)(2,1)S(1)}, bf16[128,1536]{1,0:T(8,128)(2,1)S(1)}, u32[]{:S(2)}, u32[]{:S(2)}) collective-permute-start(bf16[128,1536]{1,0:T(8,128)(2,1)S(1)} %subtract_convert_fusion), channel_id=1, source_target_pairs={{0,2},{2,0},{1,3},{3,1},{4,6},{6,4},{5,7},{7,5},{8,10},{10,8},{9,1... | collective-permute-start | bytes 1179656 | tf_op jit(solution)/shard_map/ppermute | solution.py:19
  129.0 11.2 %collective-permute-start.7 = (bf16[128,1536]{1,0:T(8,128)(2,1)S(1)}, bf16[128,1536]{1,0:T(8,128)(2,1)S(1)}, u32[]{:S(2)}, u32[]{:S(2)}) collective-permute-start(bf16[128,1536]{1,0:T(8,128)(2,1)S(1)} %subtract_convert_fusion), channel_id=1, source_target_pairs={{0,1},{1,0},{2,3},{3,2},{4,5},{5,4},{6,7},{7,6},{8,9},{9,8},{10,11... | collective-permute-start | bytes 1179656 | tf_op jit(solution)/shard_map/ppermute | solution.py:19
  138.5 3.0 collective-permute-start.6
  144.9 56.7 %reduce-scatter.42.cloned.1.call-start = ((), (), s32[]{:S(2)}) async-start(), calls=%async_computation.26 | async-start | bytes 1105920 | tf_op jit(solution)/shard_map/reduce_scatter | solution.py:70
  148.1 80.1 %reduce-scatter.32.cloned.1.call-start = ((), (), s32[]{:S(2)}) async-start(), calls=%async_computation.21 | async-start | bytes 1474560 | tf_op jit(solution)/shard_map/reduce_scatter | solution.py:70
  151.8 99.8 %reduce-scatter.50.cloned.1.call-start = ((), (), s32[]{:S(2)}) async-start(), calls=%async_computation.30 | async-start | bytes 245760 | tf_op jit(solution)/shard_map/reduce_scatter | solution.py:71
  156.6 12.3 %collective-permute-start.23 = (bf16[512,320]{0,1:T(8,128)(2,1)}, bf16[512,320]{0,1:T(8,128)(2,1)}, u32[]{:S(2)}, u32[]{:S(2)}) collective-permute-start(bf16[512,320]{0,1:T(8,128)(2,1)} %fusion.11), channel_id=1, source_target_pairs={{0,1},{1,0},{2,3},{3,2},{4,5},{5,4},{6,7},{7,6},{8,9},{9,8},{10,11... | collective-permute-start | bytes 983048 | tf_op jit(solution)/shard_map/ppermute | solution.py:19
  156.9 117.5 %reduce-scatter.46.cloned.1.call-start = ((), (), s32[]{:S(2)}) async-start(), calls=%async_computation.28 | async-start | bytes 307200 | tf_op jit(solution)/shard_map/reduce_scatter | solution.py:67
  160.5 137.0 %reduce-scatter.40.cloned.1.call-start = ((), (), s32[]{:S(2)}) async-start(), calls=%async_computation.25 | async-start | bytes 307200 | tf_op jit(solution)/shard_map/reduce_scatter | solution.py:67
  164.0 156.1 %reduce-scatter.30.cloned.1.call-start = ((), (), s32[]{:S(2)}) async-start(), calls=%async_computation.20 | async-start | bytes 307200 | tf_op jit(solution)/shard_map/reduce_scatter | solution.py:67
  166.5 35.2 %collective-permute-start.22 = (bf16[512,320]{0,1:T(8,128)(2,1)}, bf16[512,320]{0,1:T(8,128)(2,1)}, u32[]{:S(2)}, u32[]{:S(2)}) collective-permute-start(bf16[512,320]{0,1:T(8,128)(2,1)} %fusion.10), channel_id=1, source_target_pairs={{0,1},{1,0},{2,3},{3,2},{4,5},{5,4},{6,7},{7,6},{8,9},{9,8},{10,11... | collective-permute-start | bytes 983048 | tf_op jit(solution)/shard_map/ppermute | solution.py:19
  176.1 166.7 %reduce-scatter.58.cloned.1.call-start = ((), (), s32[]{:S(2)}) async-start(), calls=%async_computation.34 | async-start | bytes 276480
  178.6 49.6 %copy-start.11 = (bf16[512,384]{1,0:T(8,128)(2,1)S(1)}, bf16[512,384]{1,0:T(8,128)(2,1)}, u32[]{:S(2)}) copy-start(bf16[512,384]{1,0:T(8,128)(2,1)} %copy-done.9) | copy-start | bytes 1179652
  178.7 24.1 %collective-permute-start.24 = (bf16[512,320]{0,1:T(8,128)(2,1)}, bf16[512,320]{0,1:T(8,128)(2,1)}, u32[]{:S(2)}, u32[]{:S(2)}) collective-permute-start(bf16[512,320]{0,1:T(8,128)(2,1)} %add_convert_fusion.2), channel_id=1, source_target_pairs={{0,2},{2,0},{1,3},{3,1},{4,6},{6,4},{5,7},{7,5},{8,10},{10,8},{9,1... | collective-permute-start | bytes 983048 | tf_op jit(solution)/shard_map/ppermute | solution.py:19
  201.7 163.9 %reduce-scatter.34.cloned.1.call-start = ((), (), s32[]{:S(2)}) async-start(), calls=%async_computation.22 | async-start | bytes 368640 | tf_op jit(solution)/shard_map/reduce_scatter | solution.py:71
  232.8 87.4 %copy-start.36 = (u32[128]{0:T(128)S(1)}, u32[128]{0:T(128)}, u32[]{:S(2)}) copy-start(u32[128]{0:T(128)} %constant.88) | copy-start | bytes 1540
  233.7 87.7 %all-to-all-start.1 = ((bf16[32,2,16,320]{3,2,1,0:T(8,128)(2,1)}), bf16[32,2,16,320]{3,2,1,0:T(8,128)(2,1)S(1)}, u32[]{:S(2)}, u32[]{:S(2)}) async-start(bf16[32,2,16,320]{3,2,1,0:T(8,128)(2,1)} %copy.53), calls=%async_computation.1 | async-start | bytes 1572864 | tf_op jit(solution)/shard_map/all_to_all | solution.py:146
  241.5 141.9 %reduce-scatter.52.cloned.1.call-start = ((), (), s32[]{:S(2)}) async-start(), calls=%async_computation.31 | async-start | bytes 73728 | tf_op jit(solution)/shard_map/reduce_scatter | solution.py:72
  251.6 147.3 %reduce-scatter.60.cloned.1.call-start = ((), (), s32[]{:S(2)}) async-start(), calls=%async_computation.35 | async-start | bytes 92160
  274.5 139.9 %reduce-scatter.56.cloned.1.call-start = ((), (), s32[]{:S(2)}) async-start(), calls=%async_computation.33 | async-start | bytes 92160
  297.5 132.4 %reduce-scatter.54.cloned.1.call-start = ((), (), s32[]{:S(2)}) async-start(), calls=%async_computation.32 | async-start | bytes 92160
  320.2 125.4 %reduce-scatter.36.cloned.1.call-start = ((), (), s32[]{:S(2)}) async-start(), calls=%async_computation.23 | async-start | bytes 110592 | tf_op jit(solution)/shard_map/reduce_scatter | solution.py:72
  351.9 32.8 %collective-permute-start.25 = (bf16[12,384]{1,0:T(8,128)(2,1)S(1)}, bf16[12,384]{1,0:T(8,128)(2,1)S(1)}, u32[]{:S(2)}, u32[]{:S(2)}) collective-permute-start(bf16[12,384]{1,0:T(8,128)(2,1)S(1)} %slice.185), channel_id=1, source_target_pairs={{0,4},{1,5},{2,6},{3,7},{8,12},{9,13},{10,14},{11,15},{16,20},{17,... | collective-permute-start | bytes 27656
  (34 other events, 89.6 us)
Sparse Core Ops, SparseCore 0:
  84.0 16.6 reduce-scatter.47
  103.1 22.0 reduce-scatter.43
  127.8 23.3 reduce-scatter.37
  153.5 22.5 reduce-scatter.27
  178.5 23.1 reduce-scatter.41
  204.1 24.1 reduce-scatter.31
  230.7 20.8 reduce-scatter.49
  253.9 20.4 reduce-scatter.45
  277.0 20.4 reduce-scatter.39
  299.7 20.4 reduce-scatter.29
  322.7 20.0 reduce-scatter.57
  345.2 20.4 reduce-scatter.33
  368.0 15.3 reduce-scatter.51
  385.6 13.1 reduce-scatter.59
  401.1 13.1 reduce-scatter.55
  416.6 13.1 reduce-scatter.53
  432.1 13.3 reduce-scatter.35
